TPU v7x, 32 devices: a whole 2x2x4 slice. The times are simulated.
32 devices in a mesh: seq: 8 (over y, x, core), dp: 4 (over z).
Axes of the slice: x: 2, y: 2, z: 4, core: 2. Of those that a mesh axis runs over, the one named last changes fastest.
Arguments:
- tokens: bfloat16 [2048, 8, 512], P('seq', 'dp'), may hold values from -6 to 6
- cotangent: bfloat16 [2048, 8, 512], P('seq', 'dp'), may hold values from -6 to 6
- query_weight: bfloat16 [512, 512], replicated, may hold values from -0.5 to 0.5
- key_weight: bfloat16 [512, 512], replicated, may hold values from -0.25 to 0.25
- value_weight: bfloat16 [512, 512], replicated, may hold values from -0.25 to 0.25
- output_weight: bfloat16 [512, 512], replicated, may hold values from -2 to 2
- attn_gate_weight: bfloat16 [512, 512], replicated, may hold values from -0.25 to 0.25
- attn_gate_bias: float32 [512], replicated, may hold values from -4 to 4
- up_weight: bfloat16 [512, 2048], replicated, may hold values from -0.25 to 0.25
- down_weight: bfloat16 [2048, 512], replicated, may hold values from -0.1875 to 0.1875
- ffn_gate_weight: bfloat16 [512, 512], replicated, may hold values from -0.25 to 0.25
- ffn_gate_bias: float32 [512], replicated, may hold values from -4 to 4
- first_gain: float32 [512], replicated, may hold values from 0.5 to 1.5
- first_shift: float32 [512], replicated, may hold values from -3 to 3
- second_gain: float32 [512], replicated, may hold values from 0.5 to 1.5
- second_shift: float32 [512], replicated, may hold values from -3 to 3
- row_kind: int32 [8], P('dp'), may hold values from 1 to 2, as said below
- block_order: int32 [8, 16], P('dp'), may hold values from 0 to 15, as said below
Outputs:
- mixed: bfloat16 [2048, 8, 512], P('seq', 'dp')
- tokens_grad: bfloat16 [2048, 8, 512], P('seq', 'dp')
- query_grad: float32 [512, 512], replicated
- key_grad: float32 [512, 512], replicated
- value_grad: float32 [512, 512], replicated
- output_grad: float32 [512, 512], replicated
- attn_gate_grad: float32 [512, 512], replicated
- attn_bias_grad: float32 [512], replicated
- up_grad: float32 [512, 2048], replicated
- down_grad: float32 [2048, 512], replicated
- ffn_gate_grad: float32 [512, 512], replicated
- ffn_bias_grad: float32 [512], replicated
- first_gain_grad: float32 [512], replicated
- first_shift_grad: float32 [512], replicated
- second_gain_grad: float32 [512], replicated
- second_shift_grad: float32 [512], replicated
Inputs may be any that keep to these rules, and one draw needn't show every extreme that they name: A buffer holds one sequence of 2048 tokens where row_kind is 1, or two of 1024 tokens (positions below and from 1024) where it is 2; every draw has buffers of both kinds. `block_order`: each row is a permutation of the half-blocks; stored half-blocks 2 t and 2 t + 1 (those of the t-th device along seq) hold a half-block of the first half of the positions and one of the second half.
All inputs are finite; a program needn't handle non-finite values.
Results may differ from a plain program's by a relative error of at most 0.024.
Values may be sent and summed in bfloat16 or wider, within the bound.
A program may use at most 192 MiB of HBM per device.

v0:
```python
import math

import jax
import jax.numpy as jnp
from jax import lax
from jax.sharding import PartitionSpec as P

H = 8
HD = 64


NEG = -1e30
EPS = 1e-05


def layer_norm(values, norm_gain, norm_shift):
    average = jnp.mean(values, axis=-1, keepdims=True)
    centred = values - average
    variance = jnp.mean(centred * centred, axis=-1, keepdims=True)
    return centred * lax.rsqrt(variance + EPS) * norm_gain + norm_shift


def place_table(order_rows, kind_rows, row_start, row_count, long_len, half_len):
    row_index = row_start + jnp.arange(row_count, dtype=jnp.int32)
    slot_index = row_index // half_len
    onehot = (
        slot_index[:, None] == jnp.arange(order_rows.shape[-1], dtype=jnp.int32)[None, :]
    ).astype(jnp.int32)
    chosen = jnp.sum(order_rows[:, None, :] * onehot[None, :, :], axis=-1)
    position = chosen * half_len + row_index % half_len
    document = jnp.where(kind_rows[:, None] == 2, (position >= long_len // 2).astype(jnp.int32), 0)
    return (position, document)


def project(left, right):
    return jnp.dot(left, right, preferred_element_type=jnp.float32)


def transpose_product(left, right):
    return lax.dot_general(
        left, right, (((0,), (0,)), ((), ())), preferred_element_type=jnp.float32
    )


def times_transpose(left, right):
    return lax.dot_general(
        left, right, (((1,), (1,)), ((), ())), preferred_element_type=jnp.float32
    )


def local(
    tokens,
    cotangent,
    query_weight,
    key_weight,
    value_weight,
    output_weight,
    attn_gate_weight,
    attn_gate_bias,
    up_weight,
    down_weight,
    ffn_gate_weight,
    ffn_gate_bias,
    first_gain,
    first_shift,
    second_gain,
    second_shift,
    row_kind,
    block_order,
):
    seq_count = lax.axis_size("seq")
    here_index = lax.axis_index("seq")
    local_len, buffers, features = tokens.shape
    long_len = local_len * seq_count
    half_len = long_len // (2 * seq_count)
    flat_rows = local_len * buffers
    score_scale = 1.0 / math.sqrt(HD)
    inputs_flat = tokens.astype(jnp.float32).reshape(flat_rows, features)
    normed_one = layer_norm(inputs_flat, first_gain, first_shift).astype(jnp.bfloat16)
    query_low = (
        project(normed_one, query_weight).astype(jnp.bfloat16).reshape(local_len, buffers, H, HD)
    )
    key_low = (
        project(normed_one, key_weight).astype(jnp.bfloat16).reshape(local_len, buffers, H, HD)
    )
    value_low = (
        project(normed_one, value_weight).astype(jnp.bfloat16).reshape(local_len, buffers, H, HD)
    )
    attn_gate = jax.nn.sigmoid(project(normed_one, attn_gate_weight) + attn_gate_bias)
    key_full, value_full = (
        lax.all_gather(key_low, "seq", axis=0, tiled=True),
        lax.all_gather(value_low, "seq", axis=0, tiled=True),
    )
    query_place, query_doc = place_table(
        block_order, row_kind, here_index * local_len, local_len, long_len, half_len
    )
    all_place, all_doc = place_table(block_order, row_kind, 0, long_len, long_len, half_len)
    key_span = 512
    key_steps = long_len // key_span

    def key_scores(step_index):
        row_start = step_index * key_span
        keys_here = lax.dynamic_slice_in_dim(key_full, row_start, key_span, 0)
        raw_scores = (
            jnp.einsum("qbhd,kbhd->bhqk", query_low, keys_here, preferred_element_type=jnp.float32)
            * score_scale
        )
        key_place = lax.dynamic_slice_in_dim(all_place, row_start, key_span, 1)
        key_doc = lax.dynamic_slice_in_dim(all_doc, row_start, key_span, 1)
        allowed = (
            (key_place[:, None, :] <= query_place[:, :, None])
            & (key_doc[:, None, :] == query_doc[:, :, None])
        )[:, None]
        return (jnp.where(allowed, raw_scores, NEG), allowed, row_start, keys_here)

    def stats_step(step_index, carry):
        top_score, row_total = carry
        masked, allowed, row_start, keys_here = key_scores(step_index)
        new_top = jnp.maximum(top_score, jnp.max(masked, axis=-1))
        exp_terms = jnp.where(allowed, jnp.exp(masked - new_top[..., None]), 0.0)
        return (new_top, row_total * jnp.exp(top_score - new_top) + jnp.sum(exp_terms, axis=-1))

    start_top = jnp.full((buffers, H, local_len), NEG, jnp.float32)
    top_score, row_total = lax.fori_loop(
        0, key_steps, stats_step, (start_top, jnp.zeros_like(start_top))
    )
    log_norm = top_score + jnp.log(row_total)

    def value_step(step_index, running):
        masked, allowed, row_start, keys_here = key_scores(step_index)
        prob_low = jnp.where(allowed, jnp.exp(masked - log_norm[..., None]), 0.0).astype(
            jnp.bfloat16
        )
        values_here = lax.dynamic_slice_in_dim(value_full, row_start, key_span, 0)
        return running + jnp.einsum(
            "bhqk,kbhd->qbhd", prob_low, values_here, preferred_element_type=jnp.float32
        )

    attended = lax.fori_loop(
        0, key_steps, value_step, jnp.zeros((local_len, buffers, H, HD), jnp.float32)
    )
    attended_low = attended.astype(jnp.bfloat16).reshape(flat_rows, features)
    branch_attn = project(attended_low, output_weight)
    middle = inputs_flat + attn_gate * (branch_attn - inputs_flat)
    normed_two = layer_norm(middle, second_gain, second_shift).astype(jnp.bfloat16)
    up_pre = project(normed_two, up_weight)
    hidden_low = jax.nn.gelu(up_pre).astype(jnp.bfloat16)
    branch_ffn = project(hidden_low, down_weight)
    ffn_gate = jax.nn.sigmoid(project(normed_two, ffn_gate_weight) + ffn_gate_bias)
    output = middle + ffn_gate * (branch_ffn - middle)
    mixed = output.astype(jnp.bfloat16).reshape(local_len, buffers, features)
    grad_out = cotangent.astype(jnp.float32).reshape(flat_rows, features)
    grad_branch_ffn = (grad_out * ffn_gate).astype(jnp.bfloat16)
    ffn_pre_grad = (grad_out * (branch_ffn - middle) * ffn_gate * (1.0 - ffn_gate)).astype(
        jnp.bfloat16
    )
    grad_middle = grad_out * (1.0 - ffn_gate)
    down_grad = transpose_product(hidden_low, grad_branch_ffn)
    ffn_gate_grad = transpose_product(normed_two, ffn_pre_grad)
    ffn_bias_grad = jnp.sum(ffn_pre_grad.astype(jnp.float32), axis=0)
    grad_hidden = times_transpose(grad_branch_ffn, down_weight)
    gelu_value, gelu_back = jax.vjp(jax.nn.gelu, up_pre)
    up_pre_grad = gelu_back(grad_hidden)[0].astype(jnp.bfloat16)
    up_grad = transpose_product(normed_two, up_pre_grad)
    grad_normed_two = times_transpose(up_pre_grad, up_weight) + times_transpose(
        ffn_pre_grad, ffn_gate_weight
    )
    norm_value, norm_back = jax.vjp(layer_norm, middle, second_gain, second_shift)
    middle_part, second_gain_grad, second_shift_grad = norm_back(grad_normed_two)
    grad_middle = grad_middle + middle_part
    grad_branch_attn = (grad_middle * attn_gate).astype(jnp.bfloat16)
    attn_pre_grad = (
        grad_middle * (branch_attn - inputs_flat) * attn_gate * (1.0 - attn_gate)
    ).astype(jnp.bfloat16)
    grad_inputs = grad_middle * (1.0 - attn_gate)
    output_grad = transpose_product(attended_low, grad_branch_attn)
    attn_gate_grad = transpose_product(normed_one, attn_pre_grad)
    attn_bias_grad = jnp.sum(attn_pre_grad.astype(jnp.float32), axis=0)
    grad_attended = (
        times_transpose(grad_branch_attn, output_weight)
        .astype(jnp.bfloat16)
        .reshape(local_len, buffers, H, HD)
    )
    out_dot = jnp.einsum("qbhd,qbhd->bhq", grad_attended.astype(jnp.float32), attended)
    zero_acc = jnp.zeros((local_len, buffers, H, HD), jnp.float32)

    def grads_step(step_index, carry):
        query_acc, score_store, prob_store = carry
        masked, allowed, row_start, keys_here = key_scores(step_index)
        prob_full = jnp.where(allowed, jnp.exp(masked - log_norm[..., None]), 0.0)
        values_here = lax.dynamic_slice_in_dim(value_full, row_start, key_span, 0)
        prob_grads = jnp.einsum(
            "qbhd,kbhd->bhqk", grad_attended, values_here, preferred_element_type=jnp.float32
        )
        score_grad = (prob_full * (prob_grads - out_dot[..., None])).astype(jnp.bfloat16)
        query_acc = query_acc + jnp.einsum(
            "bhqk,kbhd->qbhd", score_grad, keys_here, preferred_element_type=jnp.float32
        )
        score_store = lax.dynamic_update_slice_in_dim(score_store, score_grad, row_start, 3)
        prob_store = lax.dynamic_update_slice_in_dim(
            prob_store, prob_full.astype(jnp.bfloat16), row_start, 3
        )
        return (query_acc, score_store, prob_store)

    empty_store = jnp.zeros((buffers, H, local_len, long_len), jnp.bfloat16)
    query_acc, score_store, prob_store = lax.fori_loop(
        0, key_steps, grads_step, (zero_acc, empty_store, empty_store)
    )
    row_count = local_len * lax.axis_size("seq")
    key_term = (
        jnp.einsum("bhqk,qbhd->kbhd", score_store, query_low, preferred_element_type=jnp.float32)
        * score_scale
    )
    value_term = jnp.einsum(
        "bhqk,qbhd->kbhd", prob_store, grad_attended, preferred_element_type=jnp.float32
    )
    summed = lax.psum_scatter(
        jnp.concatenate(
            [
                key_term.reshape(row_count, buffers, features),
                value_term.reshape(row_count, buffers, features),
            ],
            axis=2,
        ).astype(jnp.bfloat16),
        "seq",
        scatter_dimension=0,
        tiled=True,
    ).astype(jnp.float32)
    key_grad_low = summed[:, :, :features].astype(jnp.bfloat16).reshape(flat_rows, features)
    value_grad_low = summed[:, :, features:].astype(jnp.bfloat16).reshape(flat_rows, features)
    query_grad_low = (query_acc * score_scale).astype(jnp.bfloat16).reshape(flat_rows, features)
    query_grad = transpose_product(normed_one, query_grad_low)
    key_grad = transpose_product(normed_one, key_grad_low)
    value_grad = transpose_product(normed_one, value_grad_low)
    grad_normed_one = (
        times_transpose(query_grad_low, query_weight)
        + times_transpose(key_grad_low, key_weight)
        + times_transpose(value_grad_low, value_weight)
        + times_transpose(attn_pre_grad, attn_gate_weight)
    )
    first_value, first_back = jax.vjp(layer_norm, inputs_flat, first_gain, first_shift)
    inputs_part, first_gain_grad, first_shift_grad = first_back(grad_normed_one)
    tokens_grad = (
        (grad_inputs + inputs_part).astype(jnp.bfloat16).reshape(local_len, buffers, features)
    )
    (
        query_grad,
        key_grad,
        value_grad,
        output_grad,
        attn_gate_grad,
        attn_bias_grad,
        up_grad,
        down_grad,
        ffn_gate_grad,
        ffn_bias_grad,
        first_gain_grad,
        first_shift_grad,
        second_gain_grad,
        second_shift_grad,
    ) = lax.psum(
        (
            query_grad,
            key_grad,
            value_grad,
            output_grad,
            attn_gate_grad,
            attn_bias_grad,
            up_grad,
            down_grad,
            ffn_gate_grad,
            ffn_bias_grad,
            first_gain_grad,
            first_shift_grad,
            second_gain_grad,
            second_shift_grad,
        ),
        ("seq", "dp"),
    )
    return (
        mixed,
        tokens_grad,
        query_grad,
        key_grad,
        value_grad,
        output_grad,
        attn_gate_grad,
        attn_bias_grad,
        up_grad,
        down_grad,
        ffn_gate_grad,
        ffn_bias_grad,
        first_gain_grad,
        first_shift_grad,
        second_gain_grad,
        second_shift_grad,
    )


def solution(mesh):
    return jax.shard_map(
        local,
        mesh=mesh,
        in_specs=(
            P("seq", "dp", None),
            P("seq", "dp", None),
            P(),
            P(),
            P(),
            P(),
            P(),
            P(),
            P(),
            P(),
            P(),
            P(),
            P(),
            P(),
            P(),
            P(),
            P("dp"),
            P("dp", None),
        ),
        out_specs=(
            P("seq", "dp", None),
            P("seq", "dp", None),
            P(),
            P(),
            P(),
            P(),
            P(),
            P(),
            P(),
            P(),
            P(),
            P(),
            P(),
            P(),
            P(),
            P(),
        ),
        check_vma=False,
    )
```

profile of v0, /device:TPU:0, one launch (start us, length us, event | category | flops | bytes accessed | tf_op | source)
XLA Modules:
  0.0 646.9 jit_solution(9509573799137604809)
XLA Ops:
  36.8 26.3 %all-gather.5.cloned.1.call-done = bf16[2048,2,8,64]{0,3,2,1:T(8,128)(2,1)} async-done(((bf16[256,2,8,64]{0,3,2,1:T(8,128)(2,1)}), bf16[2048,2,8,64]{0,3,2,1:T(8,128)(2,1)}) %all-gather.5.cloned.1.call-update) | async-done | bytes 4194320 | tf_op jit(solution)/shard_map/all_gather | solution.py:91
  63.1 44.6 %while.48 = (s32[]{:T(128)}, f32[2,8,256]{2,1,0:T(8,128)S(1)}, f32[2,8,256]{2,1,0:T(8,128)S(1)}, s32[2,2048]{1,0:T(2,128)S(1)}, s32[2,256]{1,0:T(2,128)S(1)}, /*...) while((s32[]{:T(128)}, f32[2,8,256]{2,1,0:T(8,128)S(1)}, ...), condition=%wide.region_7.8_spmd.clone, body=%wide.region_4.7_spmd.clone.sunk | while | flops 286019584 | bytes 19378364 | solution.py:124
  63.9 6.0 fusion.150
  75.2 6.0 fusion.150
  86.1 6.1 fusion.150
  97.1 6.0 fusion.150
  107.7 24.1 %while.49 = (s32[]{:T(128)}, f32[256,2,8,64]{0,3,2,1:T(8,128)}, bf16[2048,2,8,64]{0,3,2,1:T(8,128)(2,1)}, s32[2,2048]{1,0:T(2,128)S(1)}, s32[2,256]{1,0:T(2,128)...) while((s32[]{:T(128)}, f32[256,2,8,64]{0,3,2,1:T(8,128)}, ...), condition=%wide.region_9.10_spmd.clone, body=%wide.region_8.9_spmd.clone.sunk | while | flops 548667392 | bytes 5289664 | solution.py:139
  120.0 5.8 fusion.156
  126.1 5.8 fusion.156
  167.0 5.9 broadcast_in_dim.238
  172.9 5.9 broadcast_in_dim.238.clone
  178.8 66.0 %while.50 = (s32[]{:T(128)}, f32[256,2,8,64]{0,3,2,1:T(8,128)S(1)}, bf16[2,8,256,2048]{2,3,1,0:T(8,128)(2,1)}, bf16[2,8,256,2048]{2,3,1,0:T(8,128)(2,1)}, bf16[2...) while((s32[]{:T(128)}, f32[256,2,8,64]{0,3,2,1:T(8,128)S(1)}, ...), condition=%wide.region_15.16_spmd.clone, body=%wide.region_14.15_spmd.clone.sunk | while | flops 831782912 | bytes 42809596 | solution.py:206
  185.0 7.0 %constant_dynamic-update-slice_fusion.2 = (bf16[2,8,256,2048]{2,3,1,0:T(8,128)(2,1)}, bf16[2,8,256,512]{2,3,1,0:T(8,128)(2,1)}) fusion(bf16[2,8,256,2048]{2,3,1,0:T(8,128)(2,1)} %get-tuple-element.1268, s32[]{:T(128)S(6)} %select_n.209, f32[2,8,256]{2,1,0:T(8,128)S(1)} %get-tuple-element.1297, bf16[256,2,8,64]{0,3,2,1:T(8,128)(2,1)S(1)} %copy-done.25, ...), kind=kOutput, calls=%fused_computation.47.clone.1 | convolution fusion | flops 283115520 | bytes 18646016 | tf_op jit(solution)/shard_map/while/body/eval_jaxpr/qbhd,kbhd->bhqk/dot_general | solution.py:192
  201.5 6.9 %constant_dynamic-update-slice_fusion.2 = (bf16[2,8,256,2048]{2,3,1,0:T(8,128)(2,1)}, bf16[2,8,256,512]{2,3,1,0:T(8,128)(2,1)}) fusion(bf16[2,8,256,2048]{2,3,1,0:T(8,128)(2,1)} %get-tuple-element.1268, s32[]{:T(128)S(6)} %select_n.209, f32[2,8,256]{2,1,0:T(8,128)S(1)} %get-tuple-element.1297, bf16[256,2,8,64]{0,3,2,1:T(8,128)(2,1)S(1)} %copy-done.25, ...), kind=kOutput, calls=%fused_computation.47.clone.1 | convolution fusion | flops 283115520 | bytes 18646016 | tf_op jit(solution)/shard_map/while/body/eval_jaxpr/qbhd,kbhd->bhqk/dot_general | solution.py:192
  217.9 7.0 %constant_dynamic-update-slice_fusion.2 = (bf16[2,8,256,2048]{2,3,1,0:T(8,128)(2,1)}, bf16[2,8,256,512]{2,3,1,0:T(8,128)(2,1)}) fusion(bf16[2,8,256,2048]{2,3,1,0:T(8,128)(2,1)} %get-tuple-element.1268, s32[]{:T(128)S(6)} %select_n.209, f32[2,8,256]{2,1,0:T(8,128)S(1)} %get-tuple-element.1297, bf16[256,2,8,64]{0,3,2,1:T(8,128)(2,1)S(1)} %copy-done.25, ...), kind=kOutput, calls=%fused_computation.47.clone.1 | convolution fusion | flops 283115520 | bytes 18646016 | tf_op jit(solution)/shard_map/while/body/eval_jaxpr/qbhd,kbhd->bhqk/dot_general | solution.py:192
  234.4 7.0 %constant_dynamic-update-slice_fusion.2 = (bf16[2,8,256,2048]{2,3,1,0:T(8,128)(2,1)}, bf16[2,8,256,512]{2,3,1,0:T(8,128)(2,1)}) fusion(bf16[2,8,256,2048]{2,3,1,0:T(8,128)(2,1)} %get-tuple-element.1268, s32[]{:T(128)S(6)} %select_n.209, f32[2,8,256]{2,1,0:T(8,128)S(1)} %get-tuple-element.1297, bf16[256,2,8,64]{0,3,2,1:T(8,128)(2,1)S(1)} %copy-done.25, ...), kind=kOutput, calls=%fused_computation.47.clone.1 | convolution fusion | flops 283115520 | bytes 18646016 | tf_op jit(solution)/shard_map/while/body/eval_jaxpr/qbhd,kbhd->bhqk/dot_general | solution.py:192
  244.8 10.0 %multiply_convert_fusion = bf16[2,8,64,2048]{3,2,1,0:T(8,128)(2,1)} fusion(bf16[256,2,8,64]{0,3,2,1:T(8,128)(2,1)S(1)} %get-tuple-element.1341, bf16[2,8,256,2048]{2,3,1,0:T(8,128)(2,1)} %get-tuple-element.575), kind=kOutput, calls=%fused_computation.53 | convolution fusion | flops 1077936128 | bytes 21495808 | tf_op jit(solution)/shard_map/bhqk,qbhd->kbhd/dot_general | solution.py:211
  254.8 6.4 copy.103
  261.2 10.0 %convolution_convert_fusion = bf16[2,8,64,2048]{3,2,1,0:T(8,128)(2,1)} fusion(bf16[256,2,8,64]{0,3,2,1:T(8,128)(2,1)S(1)} %copy-done.26, bf16[2,8,256,2048]{2,3,1,0:T(8,128)(2,1)} %get-tuple-element.576), kind=kOutput, calls=%fused_computation.64 | convolution fusion | flops 1075838976 | bytes 21495808 | tf_op jit(solution)/shard_map/bhqk,qbhd->kbhd/dot_general | solution.py:214
  271.1 6.2 copy.104
  277.3 7.9 %pad_maximum_fusion = bf16[2048,2,1024]{2,0,1:T(8,128)(2,1)} fusion(bf16[2048,2,512]{2,0,1:T(8,128)(2,1)} %copy.104, bf16[2048,2,512]{2,0,1:T(8,128)(2,1)} %copy.103), kind=kLoop, calls=%fused_computation.52 | loop fusion | flops 16777216 | bytes 16777216 | tf_op jit(solution)/shard_map/concatenate | solution.py:218
  312.6 43.9 %reduce-scatter.2.cloned.1.call-done = bf16[256,2,1024]{2,0,1:T(8,128)(2,1)} async-done(((bf16[2048,2,1024]{2,0,1:T(8,128)(2,1)}), bf16[256,2,1024]{2,0,1:T(8,128)(2,1)}) %reduce-scatter.2.cloned.1.call-update) | async-done | bytes 1048592 | tf_op jit(solution)/shard_map/reduce_scatter | solution.py:217
  376.3 41.5 %all-reduce = (f32[512]{0:T(512)}, f32[512]{0:T(512)}, f32[512]{0:T(512)}, f32[512]{0:T(512)}, f32[512]{0:T(512)}, /*index=5*/f32[512]{0:T(512)}) all-reduce(f32[512]{0:T(512)S(1)} %get-tuple-element.905, f32[512]{0:T(512)S(1)} %copy-done.57, f32[512]{0:T(512)S(1)} %get-tuple-element.819, ...), channel_id=1, replica_groups=mesh['seq'=8,'dp'=4] {'seq','dp'}, use_global_device_ids=true, to_apply=%region_25.26 | all-reduce | flops 3072 | bytes 24576 | tf_op jit(solution)/shard_map/psum | solution.py:261
  417.8 207.7 %all-reduce.4.cloned.1.call-done = (f32[512,512]{1,0:T(8,128)}, f32[512,512]{1,0:T(8,128)}, f32[512,512]{1,0:T(8,128)}, f32[512,512]{1,0:T(8,128)}, f32[512,512]...) async-done(((f32[512,512]{1,0:T(8,128)}, f32[512,512]{1,0:T(8,128)}, f32[512,512]{1,0:T(8,128)}, f32[512,512]{1,0:T(8,128)}, ...) | async-done | bytes 14680080 | tf_op jit(solution)/shard_map/psum | solution.py:261
  (287 shorter events, 195.5 us)
Async XLA Ops:
  7.2 138.5 %copy-start = (bf16[2048,512]{1,0:T(8,128)(2,1)S(1)}, bf16[2048,512]{1,0:T(8,128)(2,1)}, u32[]{:S(2)}) copy-start(bf16[2048,512]{1,0:T(8,128)(2,1)} %param.33) | copy-start | bytes 6291460
  7.2 55.9 %all-gather.5.cloned.1.call-start = ((), (), s32[]{:S(2)}) async-start(), calls=%async_computation.2 | async-start | bytes 4718592 | tf_op jit(solution)/shard_map/all_gather | solution.py:91
  10.1 12.7 %copy-start.5 = (f32[512,512]{1,0:T(8,128)}, f32[512,512]{1,0:T(8,128)S(1)}, u32[]{:S(2)}) copy-start(f32[512,512]{1,0:T(8,128)S(1)} %reshape.345) | copy-start | bytes 3145732
  10.1 14.5 %copy-start.32 = (f32[256,2]{1,0:T(8,128)}, f32[256,2]{1,0:T(8,128)S(1)}, u32[]{:S(2)}) copy-start(f32[256,2]{1,0:T(8,128)S(1)} %broadcast_multiply_fusion) | copy-start | bytes 6148
  12.8 11.8 %copy-start.49 = (f32[512]{0:T(512)}, f32[512]{0:T(512)S(1)}, u32[]{:S(2)}) copy-start(f32[512]{0:T(512)S(1)} %div.69) | copy-start | bytes 6148
  13.6 11.0 %copy-start.53 = (f32[512]{0:T(512)}, f32[512]{0:T(512)S(1)}, u32[]{:S(2)}) copy-start(f32[512]{0:T(512)S(1)} %add.298) | copy-start | bytes 6148
  13.7 11.0 %copy-start.51 = (f32[512]{0:T(512)}, f32[512]{0:T(512)S(1)}, u32[]{:S(2)}) copy-start(f32[512]{0:T(512)S(1)} %rsqrt.25) | copy-start | bytes 6148
  22.8 84.9 %all-gather.3.cloned.1.call-start = ((), (), s32[]{:S(2)}) async-start(), calls=%async_computation.1 | async-start | bytes 4718592 | tf_op jit(solution)/shard_map/all_gather | solution.py:92
  24.6 9.6 %copy-start.60 = (s32[2]{0:T(128)S(1)}, s32[2]{0:T(128)}, u32[]{:S(2)}) copy-start(s32[2]{0:T(128)} %param.40) | copy-start | bytes 28
  24.6 9.6 %copy-start.56 = (s32[2,16]{1,0:T(2,128)S(1)}, s32[2,16]{1,0:T(2,128)}, u32[]{:S(2)}) copy-start(s32[2,16]{1,0:T(2,128)} %param.41) | copy-start | bytes 388
  29.0 327.6 %reduce-scatter.2.cloned.1.call-start = ((), (), s32[]{:S(2)}) async-start(), calls=%async_computation.3 | async-start | bytes 9437184 | tf_op jit(solution)/shard_map/reduce_scatter | solution.py:217
  131.9 7.7 %copy-start.3 = (bf16[256,2,8,64]{0,3,2,1:T(8,128)(2,1)}, bf16[256,2,8,64]{0,3,2,1:T(8,128)(2,1)S(1)}, u32[]{:S(2)}) copy-start(bf16[256,2,8,64]{0,3,2,1:T(8,128)(2,1)S(1)} %get-tuple-element.1340) | copy-start | bytes 1572868
  131.9 9.7 %copy-start.58 = (f32[512]{0:T(512)S(1)}, f32[512]{0:T(512)}, u32[]{:S(2)}) copy-start(f32[512]{0:T(512)} %param.31) | copy-start | bytes 6148
  144.0 13.9 %copy-start.10 = (f32[512,512]{1,0:T(8,128)}, f32[512,512]{1,0:T(8,128)S(1)}, u32[]{:S(2)}) copy-start(f32[512,512]{1,0:T(8,128)S(1)} %get-tuple-element.936) | copy-start | bytes 3145732
  158.9 6.7 %copy-start.16 = (bf16[512,512]{1,0:T(8,128)(2,1)}, bf16[512,512]{1,0:T(8,128)(2,1)S(1)}, u32[]{:S(2)}) copy-start(bf16[512,512]{1,0:T(8,128)(2,1)S(1)} %multiply_convert_fusion.4) | copy-start | bytes 1572868
  254.8 6.4 copy-start.26
  285.3 340.2 %all-reduce.4.cloned.1.call-start = ((), (), s32[]{:S(2)}) async-start(), calls=%async_computation.4 | async-start | bytes 29360128 | tf_op jit(solution)/shard_map/psum | solution.py:261
  289.6 11.1 %copy-start.9 = (bf16[512,512]{1,0:T(8,128)(2,1)S(1)}, bf16[512,512]{1,0:T(8,128)(2,1)}, u32[]{:S(2)}) copy-start(bf16[512,512]{1,0:T(8,128)(2,1)} %copy-done.7) | copy-start | bytes 1572868
  289.6 11.1 %copy-start.15 = (bf16[512,512]{1,0:T(8,128)(2,1)S(1)}, bf16[512,512]{1,0:T(8,128)(2,1)}, u32[]{:S(2)}) copy-start(bf16[512,512]{1,0:T(8,128)(2,1)} %get-tuple-element.906) | copy-start | bytes 1572868
  295.7 7.9 %copy-start.28 = (bf16[512,512]{1,0:T(8,128)(2,1)S(1)}, bf16[512,512]{1,0:T(8,128)(2,1)}, u32[]{:S(2)}) copy-start(bf16[512,512]{1,0:T(8,128)(2,1)} %copy-done.27) | copy-start | bytes 1572868
  297.8 7.5 %copy-start.37 = (bf16[512,2048]{1,0:T(8,128)(2,1)S(1)}, bf16[512,2048]{1,0:T(8,128)(2,1)}, u32[]{:S(2)}) copy-start(bf16[512,2048]{1,0:T(8,128)(2,1)} %copy-done.36) | copy-start | bytes 6291460
  308.8 47.8 %copy-start.18 = (bf16[256,2,512]{0,2,1:T(8,128)(2,1)S(1)}, bf16[256,2,512]{0,2,1:T(8,128)(2,1)}, u32[]{:S(2)}) copy-start(bf16[256,2,512]{0,2,1:T(8,128)(2,1)} %copy.107) | copy-start | bytes 1572868
  625.5 6.8 %copy-start.39 = (f32[512,512]{1,0:T(8,128)S(1)}, f32[512,512]{1,0:T(8,128)}, u32[]{:S(2)}) copy-start(f32[512,512]{1,0:T(8,128)} %get-tuple-element.1308) | copy-start | bytes 3145732
  633.2 6.7 %copy-start.1 = (bf16[2048,512]{1,0:T(8,128)(2,1)S(1)}, bf16[2048,512]{1,0:T(8,128)(2,1)}, u32[]{:S(2)}) copy-start(bf16[2048,512]{1,0:T(8,128)(2,1)} %param.33) | copy-start | bytes 6291460
  (46 other events, 157.7 us)
Sparse Core Ops, SparseCore 0:
  22.9 40.1 all-gather.4
  65.6 37.4 all-gather.2
  285.4 71.0 reduce-scatter.1
  365.1 260.3 all-reduce.3
where the time goes:
time: 654 us; the launch traced here: 647 us
  waiting for transfers between devices  278 us (43%)
  matrix products  178 us (27%)
  local copies, waits for them, and re-layouts  86.8 us (13%)
  other arithmetic  46.7 us (7%)
  blocking collectives  41.5 us (6%)
  between operations  15 us (2%)
    psum x1, waiting for transfers between devices, local(): lax.psum((query_grad, key_grad, value_grad, output_grad, attn_gate_grad,...  208 us
    dot_general x8, matrix products, key_scores(): jnp.einsum('qbhd,kbhd->bhqk', query_low, keys_here, preferred_element_typ...  46.9 us
    reduce_scatter x1, waiting for transfers between devices, local(): lax.psum_scatter(jnp.concatenate([key_term.reshape(row_count, buffers, fe...  43.9 us
    psum x1, blocking collectives, local(): lax.psum((query_grad, key_grad, value_grad, output_grad, attn_gate_grad,...  41.5 us
    dot_general x4, matrix products, grads_step(): jnp.einsum('qbhd,kbhd->bhqk', grad_attended, values_here, preferred_eleme...  28 us
    all_gather x1, waiting for transfers between devices, local(): lax.all_gather(key_low, 'seq', axis=0, tiled=True)  26.3 us
    unnamed x135, local copies, waits for them, and re-layouts  26.3 us
    dot_general x4, matrix products, value_step(): jnp.einsum('bhqk,kbhd->qbhd', prob_low, values_here, preferred_element_ty...  22.7 us
  transfers between devices with their start and end apart: 4, of which 3 were waited for; matrix products, arithmetic and copies ran while one was open for 15% of the time, Pallas kernels for 0%

commit v1 on v0

v1 whole, which is shorter than its diff:
```python
import functools
import math
from types import SimpleNamespace

import jax
import jax.numpy as jnp
from jax import lax
from jax.experimental import pallas as pl
from jax.experimental.pallas import tpu as pltpu
from jax.sharding import PartitionSpec as P

H = 8
HD = 64
NEG = -1e30
EPS = 1e-05
MESH = pl.DeviceIdType.MESH
F32 = jnp.float32
BF16 = jnp.bfloat16
LANES = 128


def dot(a, b):
    return jnp.dot(a, b, preferred_element_type=F32)


def dot_nt(a, b):
    return lax.dot_general(a, b, (((1,), (1,)), ((), ())), preferred_element_type=F32)


def dot_tn(a, b):
    return lax.dot_general(a, b, (((0,), (0,)), ((), ())), preferred_element_type=F32)


def log2(value):
    return value.bit_length() - 1


def sizes(n, nd, rows, buffers, features, hidden):
    c = SimpleNamespace(n=n, nd=nd, L=rows, B=buffers, D=features, FF=hidden)
    c.T = rows * buffers
    c.N = rows * n
    c.HB = rows // 2
    c.G = n // buffers
    c.hpd = H // c.G
    c.W = c.hpd * HD
    c.QB = min(256, c.N // 2)
    c.NB = c.N // c.QB
    c.HALF = c.NB // 2
    c.FC = 512
    c.NC = hidden // c.FC
    c.LP = features // LANES
    unit = 16 * n * nd
    c.rows_a = hidden * c.LP
    c.rows_b = (hidden // LANES) * features
    c.rows_c = -(-(3 * features * c.LP) // unit) * unit
    c.used_c = 3 * features * c.LP
    c.np3 = -(-(3 * c.W) // LANES)
    c.rows_q = c.np3 * features
    c.seq_bits = log2(n)
    c.dp_bits = log2(nd)
    c.remotes = 10 * n + 2 * nd + 10 * (c.seq_bits + c.dp_bits)
    c.credits = 4 * (c.seq_bits + c.dp_bits)
    c.locals = 20 + c.NC * c.LP + hidden // LANES + 3 * c.LP + 3 * c.G
    return c


def scratch(c):
    v = pltpu.VMEM
    spaces = dict(
        tok=v((c.L, c.B * c.D), BF16),
        cot=v((c.L, c.B * c.D), BF16),
        win=v((3, c.D, LANES), BF16),
        wqkv=v((c.D, 3 * c.W), BF16),
        wg=v((c.D, c.D), BF16),
        wo=v((c.D, c.D), BF16),
        wup=v((c.D, c.FF), BF16),
        wdn=v((c.FF, c.D), BF16),
        wfg=v((c.D, c.D), BF16),
        n1=v((c.B, 2, c.HB, c.D), BF16),
        gat=v((c.n, 2, c.HB, c.D), BF16),
        nsrt=v((c.N // 2, c.D), BF16),
        qkvst=v((2 * c.n, c.HB, 3 * c.W), BF16),
        q=v((c.hpd, c.N, HD), BF16),
        k=v((c.hpd, c.N, HD), BF16),
        v=v((c.hpd, c.N, HD), BF16),
        do=v((c.hpd, c.N, HD), BF16),
        qT=v((c.W, c.N), BF16),
        vT=v((c.W, c.N), BF16),
        doT=v((c.W, c.N), BF16),
        oT=v((c.W, c.N), F32),
        dqT=v((c.W, c.N), F32),
        lseA=v((c.hpd, 1, c.N), F32),
        lseB=v((c.hpd, 1, c.N), F32),
        odot=v((c.hpd, 1, c.N), F32),
        osrt=v((2 * c.n, c.HB, c.W), BF16),
        ou=v((2 * c.n, c.HB, c.W), BF16),
        orr=v((2 * c.n, c.HB, c.W), BF16),
        dor=v((2 * c.n, c.HB, c.W), BF16),
        att=v((c.T, c.D), BF16),
        ag=v((c.T, c.D), F32),
        mid=v((c.T, c.D), F32),
        bamx=v((c.T, c.D), F32),
        acc=v((c.T, c.D), F32),
        dxr=v((c.T, c.D), F32),
        n2=v((c.T, c.D), BF16),
        n2T=v((c.D, c.T), BF16),
        gp=v((c.NC, c.T, c.FC), F32),
        hid=v((c.NC, c.T, c.FC), BF16),
        dffn=v((c.T, c.D), BF16),
        dpre=v((c.T, c.D), BF16),
        datt=v((c.T, c.D), BF16),
        dapre=v((c.T, c.D), BF16),
        wacc=v((c.D, 3 * c.W), F32),
        dns=v((2 * c.n, c.HB, c.D), BF16),
        sibs=v((2, c.n // 2, c.HB, c.D), BF16),
        sibr=v((2, c.n // 2, c.HB, c.D), BF16),
        dnr=v((c.n // 2, 2, c.HB, c.D), BF16),
        fa=v((c.rows_a, LANES), BF16),
        fb=v((c.rows_b, LANES), BF16),
        fc=v((c.rows_c, LANES), BF16),
        fq=v((c.rows_q, LANES), BF16),
        sa=v((c.rows_a, LANES), BF16),
        sb=v((c.rows_b, LANES), BF16),
        sc=v((c.rows_c, LANES), BF16),
        sq=v((c.rows_q, LANES), BF16),
        resq=v((c.G, c.rows_q, LANES), BF16),
        gqkv=v((3, c.D, c.D) if c.W < LANES else (3, 16, LANES), BF16),
        mixst=v((c.L, c.B * c.D), BF16),
        sm=v((8, c.D), F32),
        smr=v((c.n, 8, c.D), F32),
        smd=v((8, c.D), F32),
        smdr=v((c.nd, 8, c.D), F32),
        sm2=v((8, c.D), F32),
        sm2r=v((c.n, 8, c.D), F32),
        sm2d=v((8, c.D), F32),
        sm2dr=v((c.nd, 8, c.D), F32),
        ss=pltpu.SemaphoreType.DMA((c.remotes,)),
        rs=pltpu.SemaphoreType.DMA((c.remotes,)),
        ls=pltpu.SemaphoreType.DMA((c.locals,)),
        free=pltpu.SemaphoreType.REGULAR((c.credits,)),
    )
    return spaces


IN_NAMES = [
    "i_order",
    "i_kind",
    "i_bg",
    "i_bfg",
    "i_g1",
    "i_s1",
    "i_g2",
    "i_s2",
    "i_tok",
    "i_cot",
    "i_wq",
    "i_wk",
    "i_wv",
    "i_wo",
    "i_wg",
    "i_wup",
    "i_wdn",
    "i_wfg",
]
OUT_NAMES = [
    "o_mix",
    "o_tok",
    "o_q",
    "o_k",
    "o_v",
    "o_out",
    "o_ag",
    "o_up",
    "o_dn",
    "o_fg",
    "o_sm",
    "o_sm2",
]


def norm_stats(values):
    average = jnp.mean(values, axis=-1, keepdims=True)
    centred = values - average
    variance = jnp.mean(centred * centred, axis=-1, keepdims=True)
    scale = lax.rsqrt(variance + EPS)
    return centred * scale, scale


def norm_back(grad, gain, normal, scale):
    e = grad * gain
    return scale * (
        e
        - jnp.mean(e, axis=-1, keepdims=True)
        - normal * jnp.mean(e * normal, axis=-1, keepdims=True)
    )


def kernel(c, names, *refs):
    r = SimpleNamespace(**dict(zip(names, refs)))
    n, nd, L, B, D, T, N, HB, G, W = c.n, c.nd, c.L, c.B, c.D, c.T, c.N, c.HB, c.G, c.W
    QB, NB, HALF, FC, NC = c.QB, c.NB, c.HALF, c.FC, c.NC
    s = lax.axis_index("seq")
    d = lax.axis_index("dp")
    b = s // G
    g = s % G
    core = s % 2
    pair = s // 2
    pairs = n // 2
    sibling = s + 1 - 2 * core
    count = dict(remote=0, local=0, credit=0)

    def remote(src, dst, device):
        i = count["remote"]
        assert i < c.remotes
        count["remote"] += 1
        copy = pltpu.make_async_remote_copy(
            src_ref=src,
            dst_ref=dst,
            send_sem=r.ss.at[i],
            recv_sem=r.rs.at[i],
            device_id=device,
            device_id_type=MESH,
        )
        copy.start()
        return copy

    def local(src, dst):
        i = count["local"]
        assert i < c.locals
        count["local"] += 1
        copy = pltpu.make_async_copy(src, dst, r.ls.at[i])
        copy.start()
        return copy

    def at_seq(t):
        return {"seq": t, "dp": d}

    def at_dp(t):
        return {"seq": s, "dp": t}

    get_tok = local(r.i_tok, r.tok)
    window = pl.multiple_of((g * W) // LANES * LANES, LANES)
    get_win = [
        local(ref.at[:, pl.ds(window, LANES)], r.win.at[i])
        for i, ref in enumerate((r.i_wq, r.i_wk, r.i_wv))
    ]
    get_wg = local(r.i_wg, r.wg)
    get_cot = local(r.i_cot, r.cot)
    get_wo = local(r.i_wo, r.wo)
    get_wup = local(r.i_wup, r.wup)
    get_wfg = local(r.i_wfg, r.wfg)
    get_wdn = local(r.i_wdn, r.wdn)
    barrier = pltpu.get_barrier_semaphore()
    for k in range(1, n):
        pl.semaphore_signal(barrier, inc=1, device_id=at_seq((s + k) % n), device_id_type=MESH)
    for k in range(1, nd):
        pl.semaphore_signal(barrier, inc=1, device_id=at_dp((d + k) % nd), device_id_type=MESH)

    get_tok.wait()

    def inputs():
        return jnp.concatenate(
            [r.tok[:, i * D : (i + 1) * D].astype(F32) for i in range(B)], axis=0
        )

    x = inputs()
    normal, _ = norm_stats(x)
    n1 = (normal * r.i_g1[...] + r.i_s1[...]).astype(BF16)
    for i in range(B):
        r.n1[i] = n1[i * L : (i + 1) * L].reshape(2, HB, D)

    pl.semaphore_wait(barrier, n - 1 + nd - 1)

    def slot(t):
        return pl.ds(2 * t, 2)

    rows_of = r.n1
    gather = {}
    for k in range(1, pairs):
        t = 2 * ((pair + k) % pairs) + core
        gather[k] = remote(rows_of.at[t // G], r.gat.at[s], at_seq(t))
    relay = {0: remote(rows_of.at[b], r.gat.at[s], at_seq(sibling))}
    r.gat[s] = r.n1[b]

    for copy in get_win:
        copy.wait()
    if W == LANES:
        wqkv = jnp.concatenate([r.win[0], r.win[1], r.win[2]], axis=1)
    else:
        upper = (g * W) % LANES != 0
        wqkv = jnp.concatenate(
            [jnp.where(upper, r.win[i][:, W:], r.win[i][:, :W]) for i in range(3)], axis=1
        )
    r.wqkv[...] = wqkv
    get_wg.wait()
    r.ag[...] = jax.nn.sigmoid(dot(n1, r.wg[...]) + r.i_bg[...])

    order = [r.i_order[b, i] for i in range(2 * n)]
    inverse = []
    for p in range(2 * n):
        found = jnp.int32(0)
        for i in range(2 * n):
            found = jnp.where(order[i] == p, i, found)
        inverse.append(found)
    low_block = [jnp.minimum(order[2 * t], order[2 * t + 1]) for t in range(n)]
    top_block = [jnp.maximum(order[2 * t], order[2 * t + 1]) for t in range(n)]
    split = jnp.where(r.i_kind[b] == 2, F32(NEG), F32(0.0))

    def project(t):
        out = dot(r.gat[t].reshape(L, D), r.wqkv[...])
        r.qkvst[slot(t)] = (
            jnp.concatenate([out[:, :W] * (1.0 / math.sqrt(HD)), out[:, W:]], axis=1)
            .astype(BF16)
            .reshape(2, HB, 3 * W)
        )

    project(s)
    for k in range(1, pairs):
        gather[k].wait()
        u = 2 * ((pair + pairs - k) % pairs) + core
        relay[k] = remote(r.gat.at[u], r.gat.at[u], at_seq(sibling))
        project(u)
    for k in range(pairs):
        relay[k].wait()
        project(2 * ((pair + pairs - k) % pairs) + 1 - core)

    per = QB // HB
    for i in range(NB):
        at = slice(i * QB, (i + 1) * QB)
        block = jnp.concatenate([r.qkvst[inverse[i * per + m]] for m in range(per)], axis=0)
        for j, (ref, ref_t) in enumerate(((r.q, r.qT), (r.k, None), (r.v, r.vT))):
            part = block[:, j * W : (j + 1) * W]
            for h in range(c.hpd):
                ref[h, at, :] = part[:, h * HD : (h + 1) * HD]
            if ref_t is not None:
                ref_t[:, at] = part.T

    keys_at = lax.broadcasted_iota(jnp.int32, (QB, QB), 0)
    queries_at = lax.broadcasted_iota(jnp.int32, (QB, QB), 1)
    causal = keys_at <= queries_at

    def attend(blocks):
        def head(h, carry):
            hr = pl.ds(pl.multiple_of(h * HD, HD), HD)
            for i in blocks:
                at = slice(i * QB, (i + 1) * QB)
                nk = (i + 1) * QB
                scores = dot(r.k[h, 0:nk, :], r.qT[hr, at])
                diagonal = jnp.where(causal, scores[i * QB :], NEG)
                top = jnp.max(diagonal, axis=0, keepdims=True)
                low_rows = N // 2 if i >= HALF else 0
                low = scores[:low_rows] if low_rows else None
                middle = scores[low_rows : i * QB] if i * QB > low_rows else None
                if middle is not None:
                    top = jnp.maximum(top, jnp.max(middle, axis=0, keepdims=True))
                if low is not None:
                    top = jnp.maximum(top, jnp.max(low, axis=0, keepdims=True) + split)
                terms = []
                if low is not None:
                    terms.append(jnp.exp(low - (top - split)))
                if middle is not None:
                    terms.append(jnp.exp(middle - top))
                terms.append(jnp.exp(diagonal - top))
                total = sum(jnp.sum(t, axis=0, keepdims=True) for t in terms)
                weights = jnp.concatenate([t.astype(BF16) for t in terms], axis=0)
                out = dot(r.vT[hr, 0:nk], weights)
                r.oT[hr, at] = out * (1.0 / total)
                lse = top + jnp.log(total)
                r.lseB[h, :, at] = lse
                r.lseA[h, :, at] = lse - split if i >= HALF else lse
            return carry

        lax.fori_loop(0, c.hpd, head, 0)
        for i in blocks:
            r.osrt[i * per : (i + 1) * per] = (
                r.oT[:, i * QB : (i + 1) * QB].astype(BF16).T.reshape(per, HB, W)
            )

    def send_rows(which, blocks):
        for t in range(n):
            r.ou[2 * t + which] = r.osrt[blocks[t]]
        copies = []
        for k in range(1, n):
            t = (s + k) % n
            copies.append(remote(r.ou.at[2 * t + which], r.orr.at[2 * s + which], at_seq(t)))
        r.orr[2 * s + which] = r.ou[2 * s + which]
        return copies

    attend(range(HALF, NB))
    going = send_rows(1, top_block)
    attend(range(HALF))
    going += send_rows(0, low_block)

    get_wo.wait()
    get_wup.wait()
    get_wfg.wait()
    get_wdn.wait()
    get_cot.wait()
    own = [(r.i_order[i, 2 * s], r.i_order[i, 2 * s + 1]) for i in range(B)]
    which_half = [
        (jnp.where(a > z, 1, 0), jnp.where(a > z, 0, 1)) for a, z in own
    ]
    for copy in going:
        copy.wait()
    for i in range(B):
        for m in range(2):
            for j in range(G):
                r.att[i * L + m * HB : i * L + (m + 1) * HB, j * W : (j + 1) * W] = r.orr[
                    2 * (i * G + j) + which_half[i][m]
                ]
    x = inputs()
    branch = dot(r.att[...], r.wo[...]) - x
    r.bamx[...] = branch
    middle = x + r.ag[...] * branch
    r.mid[...] = middle
    normal, scale = norm_stats(middle)
    n2 = (normal * r.i_g2[...] + r.i_s2[...]).astype(BF16)
    r.n2[...] = n2
    r.n2T[...] = n2.T

    slope = math.sqrt(2.0 / math.pi)
    r.acc[...] = jnp.zeros((T, D), F32)

    def forward_chunk(j, carry):
        cols = pl.ds(pl.multiple_of(j * FC, FC), FC)
        u = dot(r.n2[...], r.wup[:, cols])
        square = u * u
        t = jnp.tanh(slope * u * (1.0 + 0.044715 * square))
        half = 0.5 * (1.0 + t)
        hidden = (u * half).astype(BF16)
        r.hid[j] = hidden
        r.gp[j] = half + 0.5 * u * (1.0 - t * t) * (slope * (1.0 + 3 * 0.044715 * square))
        r.acc[...] += dot(hidden, r.wdn[cols, :])
        return carry

    lax.fori_loop(0, NC, forward_chunk, 0)
    gate = jax.nn.sigmoid(dot(r.n2[...], r.wfg[...]) + r.i_bfg[...])
    middle = r.mid[...]
    apart = r.acc[...] - middle
    mixed = (middle + gate * apart).astype(BF16)
    for i in range(B):
        r.mixst[:, i * D : (i + 1) * D] = mixed[i * L : (i + 1) * L]
    put_mix = local(r.mixst, r.o_mix)
    grad = jnp.concatenate([r.cot[:, i * D : (i + 1) * D].astype(F32) for i in range(B)], axis=0)
    r.dffn[...] = (grad * gate).astype(BF16)
    d_pre = (grad * apart * gate * (1.0 - gate)).astype(BF16)
    r.dpre[...] = d_pre
    r.sm[0:1, :] = jnp.sum(d_pre.astype(F32), axis=0, keepdims=True)
    r.dxr[...] = grad * (1.0 - gate)
    r.acc[...] = dot_nt(d_pre, r.wfg[...])

    def backward_chunk(j, carry):
        cols = pl.ds(pl.multiple_of(j * FC, FC), FC)
        d_hidden = dot_nt(r.dffn[...], r.wdn[cols, :])
        d_up = (d_hidden * r.gp[j]).astype(BF16)
        r.gp[j] = d_up.astype(F32)
        r.acc[...] += dot_nt(d_up, r.wup[:, cols])
        return carry

    lax.fori_loop(0, NC, backward_chunk, 0)
    d_norm = r.acc[...]
    normal, scale = norm_stats(r.mid[...])
    r.sm[1:2, :] = jnp.sum(d_norm * normal, axis=0, keepdims=True)
    r.sm[2:3, :] = jnp.sum(d_norm, axis=0, keepdims=True)
    d_middle = r.dxr[...] + norm_back(d_norm, r.i_g2[...], normal, scale)
    gate = r.ag[...]
    d_att = (d_middle * gate).astype(BF16)
    d_attn_pre = (d_middle * r.bamx[...] * gate * (1.0 - gate)).astype(BF16)
    r.datt[...] = d_att
    r.dapre[...] = d_attn_pre
    r.sm[3:4, :] = jnp.sum(d_attn_pre.astype(F32), axis=0, keepdims=True)
    r.sm[4:8, :] = jnp.zeros((4, D), F32)
    r.dxr[...] = d_middle * (1.0 - gate)
    d_o = dot_nt(d_att, r.wo[...]).astype(BF16)
    for i in range(B):
        for j in range(G):
            r.ou[2 * (i * G + j) : 2 * (i * G + j) + 2] = d_o[
                i * L : (i + 1) * L, j * W : (j + 1) * W
            ].reshape(2, HB, W)
    back = []
    for k in range(1, n):
        t = (s + k) % n
        back.append(remote(r.ou.at[slot(t)], r.dor.at[slot(s)], at_seq(t)))
    r.dor[slot(s)] = r.ou[slot(s)]

    def partner(axis, bit):
        index = s if axis == "seq" else d
        mine = index // 2**bit % 2
        there = index + (1 - 2 * mine) * 2**bit
        return mine, at_seq(there) if axis == "seq" else at_dp(there)

    def add_rows(ref, start, slots, base, length):
        step = math.gcd(length, 512)

        def body(i, carry):
            at = pl.ds(pl.multiple_of(start + i * step, 16), step)
            other = slots[pl.ds(pl.multiple_of(base + i * step, 16), step), :]
            ref[at, :] = (ref[at, :].astype(F32) + other.astype(F32)).astype(BF16)
            return carry

        lax.fori_loop(0, length // step, body, 0)

    def all_reduce(ref, slots, rows, bits):
        start, length, base = jnp.int32(0), rows, 0
        trail = []
        for axis, bit in bits:
            half = length // 2
            mine, device = partner(axis, bit)
            keep = pl.multiple_of(start + mine * half, 16)
            give = pl.multiple_of(start + (1 - mine) * half, 16)
            copy = remote(ref.at[pl.ds(give, half)], slots.at[pl.ds(base, half)], device)
            yield
            copy.wait()
            credit = r.free.at[count["credit"]]
            count["credit"] += 1
            pl.semaphore_signal(credit, inc=1, device_id=device, device_id_type=MESH)
            add_rows(ref, keep, slots, base, half)
            trail.append((keep, half, device, credit))
            start, length, base = keep, half, base + half
        for keep, half, device, credit in reversed(trail):
            at = pl.ds(keep, half)
            pl.semaphore_wait(credit, 1)
            copy = remote(ref.at[at], ref.at[at], device)
            yield
            copy.wait()

    def reduce_small(own_ref, slots, dp_ref, dp_slots, out_ref):
        copies = []
        for k in range(1, n):
            copies.append(remote(own_ref, slots.at[s], at_seq((s + k) % n)))
        slots[s] = own_ref[...]
        yield
        for copy in copies:
            copy.wait()
        dp_ref[...] = sum(slots[i] for i in range(n))
        copies = []
        for k in range(1, nd):
            copies.append(remote(dp_ref, dp_slots.at[d], at_dp((d + k) % nd)))
        dp_slots[d] = dp_ref[...]
        yield
        for copy in copies:
            copy.wait()
        out_ref[...] = sum(dp_slots[i] for i in range(nd))

    running = []

    def tick():
        for job in list(running):
            if next(job, "over") == "over":
                running.remove(job)

    seq = [("seq", i) for i in range(c.seq_bits)]
    dps = [("dp", i) for i in range(c.dp_bits)]
    order_a = seq + dps
    order_b = seq[:1] + seq[1:][::-1] + dps
    order_c = seq[:1] + dps + seq[1:]

    running.append(reduce_small(r.sm, r.smr, r.smd, r.smdr, r.o_sm))

    def down_chunk(j, carry):
        part = dot_tn(r.hid[j], r.dffn[...]).astype(BF16)
        for i in range(c.LP):
            at = pl.ds(pl.multiple_of((j * c.LP + i) * FC, FC), FC)
            r.fa[at, :] = part[:, i * LANES : (i + 1) * LANES]
        return carry

    def up_chunk(j, carry):
        part = dot(r.n2T[...], r.gp[j].astype(BF16)).astype(BF16)
        for i in range(FC // LANES):
            at = pl.ds(pl.multiple_of((j * (FC // LANES) + i) * D, D), D)
            r.fb[at, :] = part[:, i * LANES : (i + 1) * LANES]
        return carry

    lax.fori_loop(0, NC, down_chunk, 0)
    running.append(all_reduce(r.fa, r.sa, c.rows_a, order_a))
    tick()
    lax.fori_loop(0, NC, up_chunk, 0)
    running.append(all_reduce(r.fb, r.sb, c.rows_b, order_b))
    tick()
    for j, part in enumerate(
        (
            dot_tn(r.att[...], r.datt[...]),
            dot_tn(r.n1[...].reshape(T, D), r.dapre[...]),
            dot(r.n2T[...], r.dpre[...]),
        )
    ):
        part = part.astype(BF16)
        for i in range(c.LP):
            at = (j * c.LP + i) * D
            r.fc[at : at + D, :] = part[:, i * LANES : (i + 1) * LANES]
    if c.rows_c > c.used_c:
        r.fc[c.used_c :, :] = jnp.zeros((c.rows_c - c.used_c, LANES), BF16)
    running.append(all_reduce(r.fc, r.sc, c.rows_c, order_c))
    tick()
    r.acc[...] = dot_nt(r.dapre[...], r.wg[...])

    for copy in back:
        copy.wait()
    for i in range(NB):
        at = slice(i * QB, (i + 1) * QB)
        block = jnp.concatenate([r.dor[inverse[i * per + m]] for m in range(per)], axis=0)
        for h in range(c.hpd):
            r.do[h, at, :] = block[:, h * HD : (h + 1) * HD]
        turned = block.T
        r.doT[:, at] = turned
        product = turned.astype(F32) * r.oT[:, at]
        for h in range(c.hpd):
            r.odot[h, :, at] = jnp.sum(product[h * HD : (h + 1) * HD], axis=0, keepdims=True)
    tick()

    def backward_block(j):
        def head(h, carry):
            hr = pl.ds(pl.multiple_of(h * HD, HD), HD)
            at = slice(j * QB, (j + 1) * QB)
            keys, values = r.k[h, at, :], r.v[h, at, :]
            keys_t = keys.T
            lse_ref = r.lseA if j < HALF else r.lseB
            weights, slopes = [], []
            for i in range(j, NB):
                to = slice(i * QB, (i + 1) * QB)
                scores = dot(keys, r.qT[hr, to])
                p = jnp.exp(scores - lse_ref[h, :, to])
                if i == j:
                    p = jnp.where(causal, p, 0.0)
                dp = dot(values, r.doT[hr, to])
                ds = (p * (dp - r.odot[h, :, to])).astype(BF16)
                weights.append(p.astype(BF16))
                slopes.append(ds)
                part = dot(keys_t, ds)
                if j == 0:
                    r.dqT[hr, to] = part
                else:
                    r.dqT[hr, to] += part
            weights = jnp.concatenate(weights, axis=1)
            slopes = jnp.concatenate(slopes, axis=1)
            r.v[h, at, :] = dot(weights, r.do[h, j * QB :, :]).astype(BF16)
            r.k[h, at, :] = dot(slopes, r.q[h, j * QB :, :]).astype(BF16)
            return carry

        lax.fori_loop(0, c.hpd, head, 0)

    def finish_half(which, blocks):
        for i in blocks:
            at = slice(i * QB, (i + 1) * QB)
            parts = [(r.dqT[:, at] * (1.0 / math.sqrt(HD))).astype(BF16).T]
            parts += [r.k[h, at, :] for h in range(c.hpd)]
            parts += [r.v[h, at, :] for h in range(c.hpd)]
            rows = jnp.concatenate(parts, axis=1)
            r.qkvst[i * per : (i + 1) * per] = rows.reshape(per, HB, 3 * W)
            r.dns[i * per : (i + 1) * per] = (
                dot_nt(rows, r.wqkv[...]).astype(BF16).reshape(per, HB, D)
            )
        table = top_block if which else low_block

        def pick(m, parity):
            return jnp.where(parity == 0, table[2 * m], table[2 * m + 1])

        for m in range(pairs):
            r.sibs[which, m] = r.dns[pick(m, 1 - core)]
        return remote(r.sibs.at[which], r.sibr.at[which], at_seq(sibling)), pick

    def pass_on(which, copy, pick):
        copy.wait()
        for m in range(pairs):
            r.sibs[which, m] = (
                r.dns[pick(m, core)].astype(F32) + r.sibr[which, m].astype(F32)
            ).astype(BF16)
        copies = []
        for k in range(1, pairs):
            m = (pair + k) % pairs
            copies.append(
                remote(r.sibs.at[which, m], r.dnr.at[pair, which], at_seq(2 * m + core))
            )
        r.dnr[pair, which] = r.sibs[which, pair]
        return copies

    for j in range(HALF):
        backward_block(j)
        tick()
    low_copy, low_pick = finish_half(0, range(HALF))

    def weight_part(which):
        for i in range(n):
            at = inverse[which * n + i]
            r.nsrt[i * HB : (i + 1) * HB, :] = r.gat[at // 2, at % 2]
        return dot_tn(
            r.nsrt[...], r.qkvst[which * n : (which + 1) * n].reshape(N // 2, 3 * W)
        )

    r.wacc[...] = weight_part(0)
    arriving = pass_on(0, low_copy, low_pick)
    for j in range(HALF, NB):
        backward_block(j)
        tick()
    top_copy, top_pick = finish_half(1, range(HALF, NB))
    part = (r.wacc[...] + weight_part(1)).astype(BF16)
    if c.np3 * LANES > 3 * W:
        part = jnp.concatenate([part, jnp.zeros((D, c.np3 * LANES - 3 * W), BF16)], axis=1)
    for i in range(c.np3):
        r.fq[i * D : (i + 1) * D, :] = part[:, i * LANES : (i + 1) * LANES]
    arriving += pass_on(1, top_copy, top_pick)

    group_bits = log2(G)

    def heads_reduce():
        yield from all_reduce(
            r.fq, r.sq, c.rows_q, [("seq", i) for i in range(group_bits, c.seq_bits)] + dps
        )
        r.resq[g] = r.fq[...]
        held = [g]
        for bit in reversed(range(group_bits)):
            mine, device = partner("seq", bit)
            copies = [remote(r.resq.at[i], r.resq.at[i], device) for i in held]
            yield
            for copy in copies:
                copy.wait()
            held = held + [i + (1 - 2 * mine) * 2**bit for i in held]

    running.append(heads_reduce())
    tick()

    for copy in arriving:
        copy.wait()
    parts = []
    for i in range(B):
        for m in range(2):
            parts.append(
                sum(
                    r.dnr[i * (G // 2) + j, which_half[i][m]].astype(F32) for j in range(G // 2)
                )
            )
    d_norm = jnp.concatenate(parts, axis=0) + r.acc[...]
    normal, scale = norm_stats(inputs())
    r.sm2[0:1, :] = jnp.sum(d_norm * normal, axis=0, keepdims=True)
    r.sm2[1:2, :] = jnp.sum(d_norm, axis=0, keepdims=True)
    r.sm2[2:8, :] = jnp.zeros((6, D), F32)
    running.append(reduce_small(r.sm2, r.sm2r, r.sm2d, r.sm2dr, r.o_sm2))
    tick()
    put_mix.wait()
    grads = (r.dxr[...] + norm_back(d_norm, r.i_g1[...], normal, scale)).astype(BF16)
    for i in range(B):
        r.mixst[:, i * D : (i + 1) * D] = grads[i * L : (i + 1) * L]
    puts = [local(r.mixst, r.o_tok)]
    while running:
        tick()

    for j in range(NC):
        for i in range(c.LP):
            at = (j * c.LP + i) * FC
            puts.append(
                local(
                    r.fa.at[at : at + FC],
                    r.o_dn.at[j * FC : (j + 1) * FC, i * LANES : (i + 1) * LANES],
                )
            )
    for i in range(c.FF // LANES):
        puts.append(
            local(r.fb.at[i * D : (i + 1) * D], r.o_up.at[:, i * LANES : (i + 1) * LANES])
        )
    for j, ref in enumerate((r.o_out, r.o_ag, r.o_fg)):
        for i in range(c.LP):
            at = (j * c.LP + i) * D
            puts.append(local(r.fc.at[at : at + D], ref.at[:, i * LANES : (i + 1) * LANES]))
    outs = (r.o_q, r.o_k, r.o_v)
    for i in range(G):
        if W == LANES:
            for j, ref in enumerate(outs):
                puts.append(
                    local(
                        r.resq.at[i, j * D : (j + 1) * D], ref.at[:, i * LANES : (i + 1) * LANES]
                    )
                )
            continue
        block = jnp.concatenate(
            [r.resq[i, m * D : (m + 1) * D, :] for m in range(c.np3)], axis=1
        )
        for j in range(3):
            r.gqkv[j, :, i * W : (i + 1) * W] = block[:, j * W : (j + 1) * W]
    if W < LANES:
        for j, ref in enumerate(outs):
            puts.append(local(r.gqkv.at[j], ref))
    for put in puts:
        put.wait()


def solution(mesh):
    n, nd = mesh.shape["seq"], mesh.shape["dp"]

    def local(
        tokens,
        cotangent,
        query_weight,
        key_weight,
        value_weight,
        output_weight,
        attn_gate_weight,
        attn_gate_bias,
        up_weight,
        down_weight,
        ffn_gate_weight,
        ffn_gate_bias,
        first_gain,
        first_shift,
        second_gain,
        second_shift,
        row_kind,
        block_order,
    ):
        L, B, D = tokens.shape
        FF = up_weight.shape[1]
        c = sizes(n, nd, L, B, D, FF)
        spaces = scratch(c)
        names = IN_NAMES + OUT_NAMES + list(spaces)
        smem = pl.BlockSpec(memory_space=pltpu.SMEM)
        vmem = pl.BlockSpec(memory_space=pltpu.VMEM)
        hbm = pl.BlockSpec(memory_space=pl.ANY)

        def shape(*dims, dtype=BF16):
            return jax.ShapeDtypeStruct(dims, dtype)

        def row(vector):
            return vector.reshape(1, -1)

        out = pl.pallas_call(
            functools.partial(kernel, c, names),
            out_shape=(
                shape(L, B * D),
                shape(L, B * D),
                shape(D, D),
                shape(D, D),
                shape(D, D),
                shape(D, D),
                shape(D, D),
                shape(D, FF),
                shape(FF, D),
                shape(D, D),
                shape(8, D, dtype=F32),
                shape(8, D, dtype=F32),
            ),
            in_specs=[smem] * 2 + [vmem] * 6 + [hbm] * 10,
            out_specs=(hbm,) * 10 + (vmem,) * 2,
            scratch_shapes=list(spaces.values()),
            compiler_params=pltpu.CompilerParams(
                collective_id=0, has_side_effects=True, vmem_limit_bytes=VMEM_BYTES
            ),
            name="layer",
        )(
            block_order,
            row_kind,
            row(attn_gate_bias),
            row(ffn_gate_bias),
            row(first_gain),
            row(first_shift),
            row(second_gain),
            row(second_shift),
            tokens.reshape(L, B * D),
            cotangent.reshape(L, B * D),
            query_weight,
            key_weight,
            value_weight,
            output_weight,
            attn_gate_weight,
            up_weight,
            down_weight,
            ffn_gate_weight,
        )
        mix, tok, dq, dk, dv, dout, dag, dup, ddn, dfg, small, small2 = out
        wide = [a.astype(F32) for a in (dq, dk, dv, dout, dag, dup, ddn, dfg)]
        return (
            mix.reshape(L, B, D),
            tok.reshape(L, B, D),
            wide[0],
            wide[1],
            wide[2],
            wide[3],
            wide[4],
            small[3],
            wide[5],
            wide[6],
            wide[7],
            small[0],
            small2[0],
            small2[1],
            small[1],
            small[2],
        )

    sharded = P("seq", "dp", None)
    return jax.shard_map(
        local,
        mesh=mesh,
        in_specs=(sharded, sharded) + (P(),) * 14 + (P("dp"), P("dp", None)),
        out_specs=(sharded, sharded) + (P(),) * 14,
        check_vma=False,
    )


VMEM_BYTES = 63 * 2**20
```

time: 654 us -> 252 us (0.39); the launches traced: 647 us -> 251 us
  waiting for transfers between devices: 278 us -> 0 us
  Pallas kernels: 0 us -> 230 us
  matrix products: 178 us -> 0 us
  local copies, waits for them, and re-layouts: 86.8 us -> 7.66 us
  blocking collectives: 41.5 us -> 0 us
  other arithmetic: 46.7 us -> 13.5 us
  between operations: 15 us -> 0.67 us
    pallas_call x0 -> x1, Pallas kernels: none -> 230 us  [local(): pl.pallas_call(functools.partial(kernel, c, names), out_shape=(shape(L, B...]
    psum x1 -> x0, waiting for transfers between devices: 208 us -> none  [local(): lax.psum((query_grad, key_grad, value_grad, output_grad, attn_gate_grad,...]
    dot_general x46 -> x0, matrix products: 178 us -> none  [the longest x8 46.9 us: key_scores(): jnp.einsum('qbhd,kbhd->bhqk', query_low, keys_here, preferred_element_typ...]
    reduce_scatter x1 -> x0, waiting for transfers between devices: 43.9 us -> none  [local(): lax.psum_scatter(jnp.concatenate([key_term.reshape(row_count, buffers, fe...]
    psum x1 -> x0, blocking collectives: 41.5 us -> none  [local(): lax.psum((query_grad, key_grad, value_grad, output_grad, attn_gate_grad,...]
    reshape x16 -> x2, local copies, waits for them, and re-layouts: 35.9 us -> 2.33 us  [the longest x1 1.17 us: local(): mix.reshape(L, B, D)]
    all_gather x2 -> x0, waiting for transfers between devices: 26.4 us -> none  [the longest x1 26.3 us: local(): lax.all_gather(key_low, 'seq', axis=0, tiled=True)]
    reduce_sum x12 -> x0, other arithmetic: 25 us -> none  [the longest x4 18.3 us: stats_step(): jnp.sum(exp_terms, axis=-1)]
  transfers between devices with their start and end apart: 4 -> 0, of which waited for: 3 -> 0; matrix products, arithmetic and copies ran while one was open for 15% -> 0% of each run, Pallas kernels for 0% -> 0%
where the time goes in v1:
time: 252 us; the launch traced here: 251 us
  Pallas kernels  230 us (91%)
  other arithmetic  13.5 us (5%)
  local copies, waits for them, and re-layouts  7.66 us (3%)
    pallas_call x1, Pallas kernels, local(): pl.pallas_call(functools.partial(kernel, c, names), out_shape=(shape(L, B...  230 us
    convert_element_type x8, other arithmetic, local(): wide = [a.astype(F32) for a in (dq, dk, dv, dout, dag, dup, ddn, dfg)]  13.5 us

profile of v1, /device:TPU:0, one launch (start us, length us, event | category | flops | bytes accessed | tf_op | source)
XLA Modules:
  0.0 251.5 jit_solution(16196015249052389625)
XLA Ops:
  0.6 1.9 copy.34
  2.6 1.9 copy.35
  4.5 229.7 %layer.1 = (bf16[256,1024]{1,0:T(8,128)(2,1)}, bf16[256,1024]{1,0:T(8,128)(2,1)}, bf16[512,512]{1,0:T(8,128)(2,1)}, bf16[512,512]{1,0:T(8,128)(2,1)}, bf16[512,5...) custom-call(s32[2,16]{1,0:T(2,128)} %refs_0_.1, ...), custom_call_target="tpu_custom_call" | custom-call | tf_op jit(solution)/shard_map/layer/pallas_call | solution.py:824
  234.1 1.5 fusion
  235.6 0.0 copy-start
  235.6 4.3 %convert_element_type.29 = f32[512,2048]{1,0:T(8,128)} convert(bf16[512,2048]{1,0:T(8,128)(2,1)} %get-tuple-element.36) | non-fusion elementwise | flops 1048576 | bytes 6291456 | tf_op jit(solution)/shard_map/convert_element_type | solution.py:868
  239.9 0.0 copy-done
  239.9 2.6 %convert_element_type.30 = f32[2048,512]{1,0:T(8,128)} convert(bf16[2048,512]{1,0:T(8,128)(2,1)S(1)} %copy-done) | non-fusion elementwise | flops 1048576 | bytes 6291456 | tf_op jit(solution)/shard_map/convert_element_type | solution.py:868
  242.5 0.0 copy-done.6
  242.5 1.1 convert_element_type.24
  243.6 0.0 copy-done.5
  243.6 1.1 convert_element_type.25
  244.7 0.0 copy-done.4
  244.7 1.1 convert_element_type.26
  245.8 0.0 copy-done.3
  245.8 1.1 convert_element_type.27
  246.9 0.0 copy-done.2
  246.9 1.1 convert_element_type.28
  248.0 0.0 copy-done.1
  248.0 1.1 convert_element_type.31
  249.1 0.0 copy-done.8
  249.2 1.2 reshape.70
  250.3 0.0 copy-done.7
  250.3 1.2 reshape.71
  (8 shorter events, 0.0 us)
Async XLA Ops:
  235.6 4.3 %copy-start = (bf16[2048,512]{1,0:T(8,128)(2,1)S(1)}, bf16[2048,512]{1,0:T(8,128)(2,1)}, u32[]{:S(2)}) copy-start(bf16[2048,512]{1,0:T(8,128)(2,1)} %get-tuple-element.37) | copy-start | bytes 6291460
  239.9 2.6 %copy-start.6 = (bf16[512,512]{1,0:T(8,128)(2,1)S(1)}, bf16[512,512]{1,0:T(8,128)(2,1)}, u32[]{:S(2)}) copy-start(bf16[512,512]{1,0:T(8,128)(2,1)} %get-tuple-element.30) | copy-start | bytes 1572868
  239.9 3.7 %copy-start.5 = (bf16[512,512]{1,0:T(8,128)(2,1)S(1)}, bf16[512,512]{1,0:T(8,128)(2,1)}, u32[]{:S(2)}) copy-start(bf16[512,512]{1,0:T(8,128)(2,1)} %get-tuple-element.31) | copy-start | bytes 1572868
  242.5 2.2 copy-start.4
  242.5 3.3 %copy-start.3 = (bf16[512,512]{1,0:T(8,128)(2,1)S(1)}, bf16[512,512]{1,0:T(8,128)(2,1)}, u32[]{:S(2)}) copy-start(bf16[512,512]{1,0:T(8,128)(2,1)} %get-tuple-element.33) | copy-start | bytes 1572868
  243.6 3.3 %copy-start.2 = (bf16[512,512]{1,0:T(8,128)(2,1)S(1)}, bf16[512,512]{1,0:T(8,128)(2,1)}, u32[]{:S(2)}) copy-start(bf16[512,512]{1,0:T(8,128)(2,1)} %get-tuple-element.34) | copy-start | bytes 1572868
  244.7 3.3 %copy-start.1 = (bf16[512,512]{1,0:T(8,128)(2,1)S(1)}, bf16[512,512]{1,0:T(8,128)(2,1)}, u32[]{:S(2)}) copy-start(bf16[512,512]{1,0:T(8,128)(2,1)} %get-tuple-element.38) | copy-start | bytes 1572868
  245.8 3.3 %copy-start.8 = (bf16[256,1024]{1,0:T(8,128)(2,1)S(1)}, bf16[256,1024]{1,0:T(8,128)(2,1)}, u32[]{:S(2)}) copy-start(bf16[256,1024]{1,0:T(8,128)(2,1)} %get-tuple-element.28) | copy-start | bytes 1572868
  246.9 3.4 %copy-start.7 = (bf16[256,1024]{1,0:T(8,128)(2,1)S(1)}, bf16[256,1024]{1,0:T(8,128)(2,1)}, u32[]{:S(2)}) copy-start(bf16[256,1024]{1,0:T(8,128)(2,1)} %get-tuple-element.29) | copy-start | bytes 1572868
